TPU v7x, 32 devices: a whole 2x2x4 slice. The times are simulated.
32 devices in a mesh: parts: 2 (over y), expert: 4 (over z), hidden: 2 (over x), rep: 2 (over core).
Axes of the slice: x: 2, y: 2, z: 4, core: 2. Of those that a mesh axis runs over, the one named last changes fastest.
Arguments:
- tokens: bfloat16 [1024, 4096], P(('parts', 'expert', 'rep'), 'hidden'), parts along dimension 0, may hold values from -6 to 6
- route_ids: int32 [1024, 2], P(('parts', 'expert', 'rep')), parts along dimension 0, may hold values from 0 to 3, all different within a row; in each aligned block of 64 rows (0 to 63, 64 to 127, ...) at most 48 rows name the same one
- route_weight: float32 [1024, 2], P(('parts', 'expert', 'rep')), parts along dimension 0, may hold values from 0.1 to 1
- user_slot: int32 [128, 4], P(('parts', 'expert', 'rep')), parts along dimension 0, may hold values from 0 to 15
- gate_weight: bfloat16 [4, 4096, 1536], P('expert', None, 'hidden'), may hold values from -0.09375 to 0.09375
- up_weight: bfloat16 [4, 4096, 1536], P('expert', None, 'hidden'), may hold values from -0.09375 to 0.09375
- down_weight: bfloat16 [4, 1536, 4096], P('expert', 'hidden'), may hold values from -0.15625 to 0.15625
- adapter_down: bfloat16 [4, 4096, 128], P('expert', 'hidden'), may hold values from -0.09375 to 0.09375
- adapter_up: bfloat16 [4, 128, 1536], P('expert', None, 'hidden'), may hold values from -2 to 2
Outputs:
- mixed: bfloat16 [1024, 4096], P(('parts', 'expert', 'rep'), 'hidden'), parts along dimension 0
There are 2 independent parts, one for each index of `parts`. A program takes and returns all parts, laid end to end along the dimension named above; an argument that names none is the same for every part. Nothing has to cross between parts.
Inputs may be any that keep to these rules, and one draw needn't show every extreme that they name: `route_ids`: each row names 2 different experts. Among the 64 rows of one device (aligned blocks), no expert is named by more than 48 rows, a bound that some block reaches.
All inputs are finite; a program needn't handle non-finite values.
Results may differ from a plain program's by a relative error of at most 0.015.
Values may be sent and summed in bfloat16 or wider, within the bound.
A program may use at most 64 MiB of HBM per device.

v0:
```python
import jax
import jax.numpy as jnp
from jax import lax
from jax.sharding import PartitionSpec as P

RANK = 8
USER_TOK = 8


def local(
    tokens,
    route_ids,
    route_weight,
    user_slot,
    gate_weight,
    up_weight,
    down_weight,
    adapter_down,
    adapter_up,
):
    experts = lax.axis_size("expert")
    tok_rows, choices_each = route_ids.shape
    expert_capacity = tok_rows * choices_each * 3 // (2 * experts)
    width = gate_weight.shape[1]
    shard_width = tokens.shape[1]
    adapt_cols = adapter_down.shape[2]
    source_rows = lax.all_gather(tokens, "hidden", axis=1, tiled=True)
    sent_width = source_rows.shape[1]
    flat_ids = route_ids.reshape(-1)
    choose = (flat_ids[:, None] == jnp.arange(experts)[None, :]).astype(jnp.int32)
    position = jnp.sum((jnp.cumsum(choose, axis=0) - 1) * choose, axis=1)
    slot_index = flat_ids * expert_capacity + position
    dispatch = slot_index[:, None] == jnp.arange(experts * expert_capacity)[None, :]
    token_of = jnp.arange(tok_rows * choices_each) // choices_each
    owning = token_of[:, None] == jnp.arange(tok_rows)[None, :]
    send_map = jnp.dot(
        dispatch.T.astype(jnp.bfloat16),
        owning.astype(jnp.bfloat16),
        preferred_element_type=jnp.float32,
    ).astype(jnp.bfloat16)
    send_rows = (
        jnp.dot(send_map, source_rows, preferred_element_type=jnp.float32)
        .astype(jnp.bfloat16)
        .reshape(experts, expert_capacity, sent_width)
    )
    user_of = token_of // USER_TOK
    user_pick = user_of[:, None] == jnp.arange(user_slot.shape[0])[None, :]
    user_rows = jnp.sum(jnp.where(user_pick[:, :, None], user_slot[None, :, :], 0), axis=1)
    slot_code = jnp.sum(choose * user_rows, axis=1)
    send_codes = (
        jnp.sum(jnp.where(dispatch, slot_code[:, None], 0), axis=0)
        .astype(jnp.bfloat16)
        .reshape(experts, expert_capacity)
    )
    factor_full = lax.all_gather(adapter_down[0], "hidden", axis=0, tiled=True)
    rows = lax.all_to_all(send_rows, "expert", split_axis=0, concat_axis=0, tiled=True)
    codes = lax.all_to_all(send_codes, "expert", split_axis=0, concat_axis=0, tiled=True)
    sources = rows.shape[0]
    per_source = rows.shape[1]
    flattened = rows.reshape(sources * per_source, width)
    gate_values = jnp.dot(flattened, gate_weight[0], preferred_element_type=jnp.float32)
    up_values = jnp.dot(flattened, up_weight[0], preferred_element_type=jnp.float32)
    rank_full = jnp.dot(flattened, factor_full, preferred_element_type=jnp.float32)
    slot_mask = (
        codes.reshape(-1).astype(jnp.int32)[:, None] == (jnp.arange(adapt_cols) // RANK)[None, :]
    )
    rank_portion = jnp.where(slot_mask, rank_full, 0.0).astype(jnp.bfloat16)
    up_values = up_values + jnp.dot(rank_portion, adapter_up[0], preferred_element_type=jnp.float32)
    hidden_act = (jax.nn.silu(gate_values) * up_values).astype(jnp.bfloat16)
    partial_value = jnp.dot(hidden_act, down_weight[0], preferred_element_type=jnp.float32).reshape(
        sources, per_source, width
    )
    result = lax.psum_scatter(
        partial_value.astype(jnp.bfloat16), "hidden", scatter_dimension=2, tiled=True
    ).astype(jnp.float32)
    returned = lax.all_to_all(
        result.astype(jnp.bfloat16), "expert", split_axis=0, concat_axis=0, tiled=True
    ).astype(result.dtype)
    picked = jnp.take(
        returned.reshape(experts * expert_capacity, shard_width), slot_index, axis=0
    ).reshape(tok_rows, choices_each, shard_width)
    mixed = jnp.sum(picked * route_weight[:, :, None], axis=1)
    return mixed.astype(jnp.bfloat16)


def solution(mesh):
    in_specs = (
        P(("parts", "expert", "rep"), "hidden"),
        P(("parts", "expert", "rep"), None),
        P(("parts", "expert", "rep"), None),
        P(("parts", "expert", "rep"), None),
        P("expert", None, "hidden"),
        P("expert", None, "hidden"),
        P("expert", "hidden", None),
        P("expert", "hidden", None),
        P("expert", None, "hidden"),
    )
    out_specs = P(("parts", "expert", "rep"), "hidden")
    return jax.shard_map(local, mesh=mesh, in_specs=in_specs, out_specs=out_specs, check_vma=False)
```

profile of v0, /device:TPU:0, one launch (start us, length us, event | category | flops | bytes accessed | tf_op | source)
XLA Modules:
  0.0 145.6 jit_solution(6415885413791973828)
XLA Ops:
  6.5 0.0 copy-start
  6.5 0.8 copy.28
  7.4 0.1 reshape.157
  7.5 0.1 fusion.16
  7.6 0.8 select_reduce_fusion.3
  8.4 0.1 copy.31
  8.5 0.2 reduce_window_sum.11
  8.7 0.2 select_reduce_fusion.1
  8.8 0.1 select_reduce_fusion
  9.0 0.7 convert_element_type.62
  9.6 6.3 %all-to-all-start.1 = ((bf16[4,1,48]{2,1,0:T(2,128)(2,1)}), bf16[4,1,48]{2,1,0:T(2,128)(2,1)S(1)}, u32[]{:S(2)}, u32[]{:S(2)}) async-start(bf16[4,1,48]{2,1,0:T(2,128)(2,1)} %convert_element_type.62), calls=%async_computation.1 | async-start | bytes 4096 | tf_op jit(solution)/shard_map/all_to_all | solution.py:57
  16.0 8.6 %all_gather.6 = bf16[64,4096]{1,0:T(8,128)(2,1)S(1)} all-gather(bf16[64,2048]{1,0:T(8,128)(2,1)} %param.9), channel_id=1, replica_groups=mesh['parts'=2,'expert'=4,'hidden'=2,'rep'=2] {'hidden'}, dimensions={1}, use_global_device_ids=true | all-gather | bytes 786432 | tf_op jit(solution)/shard_map/all_gather | solution.py:27
  24.6 2.0 %convolution_convert_fusion = bf16[192,4096]{1,0:T(8,128)(2,1)} fusion(bf16[64,4096]{1,0:T(8,128)(2,1)S(1)} %all_gather.6, s32[128]{0:T(128)S(1)} %get-tuple-element.8, s32[128]{0:T(128)S(1)} %get-tuple-element.7), kind=kOutput, calls=%fused_computation.8 | convolution fusion | flops 104640512 | bytes 2098176 | tf_op jit(solution)/shard_map/dot_general | solution.py:42
  26.7 0.0 all-to-all-done.1
  26.7 4.8 %all-to-all-start = ((bf16[4,48,4096]{2,1,0:T(8,128)(2,1)}), bf16[4,48,4096]{2,1,0:T(8,128)(2,1)S(1)}, u32[]{:S(2)}, u32[]{:S(2)}) async-start(bf16[4,48,4096]{2,1,0:T(8,128)(2,1)} %bitcast), calls=%async_computation | async-start | bytes 3145728 | tf_op jit(solution)/shard_map/all_to_all | solution.py:56
  31.5 0.0 all-gather.3.cloned.1.call-start
  31.5 0.7 all-gather.3.cloned.1.call-update
  32.2 0.0 reduce-scatter.2.cloned.1.call-start
  32.3 0.1 reshape.162
  32.4 34.6 %all-to-all-done = bf16[4,48,4096]{2,1,0:T(8,128)(2,1)S(1)} async-done(((bf16[4,48,4096]{2,1,0:T(8,128)(2,1)}), bf16[4,48,4096]{2,1,0:T(8,128)(2,1)S(1)}, u32[]{:S(2)}, u32[]{:S(2)}) %all-to-all-start) | async-done | bytes 1572896 | tf_op jit(solution)/shard_map/all_to_all | solution.py:56
  66.9 4.2 %fusion.2 = f32[192,768]{1,0:T(8,128)S(1)} fusion(bf16[192,4096]{1,0:T(8,128)(2,1)S(1)} %bitcast.36, bf16[1,4096,768]{2,1,0:T(8,128)(2,1)} %param.14), kind=kOutput, calls=%fused_computation.3 | convolution fusion | flops 1207959552 | bytes 8454144 | tf_op jit(solution)/shard_map/dot_general | solution.py:62
  71.1 5.0 %fusion.4 = f32[192,768]{1,0:T(8,128)} fusion(bf16[192,4096]{1,0:T(8,128)(2,1)S(1)} %bitcast.37, bf16[1,4096,768]{2,1,0:T(8,128)(2,1)} %param.13), kind=kOutput, calls=%fused_computation.5 | convolution fusion | flops 1207959552 | bytes 8454144 | tf_op jit(solution)/shard_map/dot_general | solution.py:61
  76.1 0.0 all-gather.3.cloned.1.call-done
  76.1 0.0 copy-done
  76.1 2.2 %fusion.10 = bf16[192,768]{1,0:T(8,128)(2,1)S(1)} fusion(f32[192,768]{1,0:T(8,128)S(1)} %fusion.2, bf16[192,4096]{1,0:T(8,128)(2,1)S(1)} %bitcast.38, bf16[1,4096,128]{2,1,0:T(8,128)(2,1)} %all-gather.3.cloned.1.call-done, f32[192,768]{1,0:T(8,128)} %fusion.4, bf16[1,128,768]{2,1,0:T(8,128)(2,1)S(1)} %copy-done, s32[128]{0:T(128)S(1)} %and_select_fusion, ...), kind=kOutput, calls=%fused_computation.11 | convolution fusion | flops 240181248 | bytes 4293888 | tf_op jit(solution)/shard_map/dot_general | solution.py:68
  78.3 5.3 %fusion.6 = bf16[4,48,4096]{2,1,0:T(8,128)(2,1)} fusion(bf16[4,48,768]{2,1,0:T(8,128)(2,1)S(1)} %bitcast.39, bf16[1,768,4096]{2,1,0:T(8,128)(2,1)} %param.15), kind=kOutput, calls=%fused_computation.7 | convolution fusion | flops 1208745984 | bytes 8159232 | tf_op jit(solution)/shard_map/dot_general | solution.py:70
  83.6 0.0 copy-start.1
  83.6 0.0 copy-start.2
  83.6 0.0 reduce-scatter.2.cloned.1.call-update
  83.7 25.3 %reduce-scatter.2.cloned.1.call-done = bf16[4,48,2048]{2,1,0:T(8,128)(2,1)} async-done(((bf16[4,48,4096]{2,1,0:T(8,128)(2,1)}), bf16[4,48,2048]{2,1,0:T(8,128)(2,1)}) %reduce-scatter.2.cloned.1.call-update) | async-done | bytes 786448 | tf_op jit(solution)/shard_map/reduce_scatter | solution.py:73
  109.0 4.6 %all-to-all-start.2 = ((bf16[4,48,2048]{2,1,0:T(8,128)(2,1)}), bf16[4,48,2048]{2,1,0:T(8,128)(2,1)S(1)}, u32[]{:S(2)}, u32[]{:S(2)}) async-start(bf16[4,48,2048]{2,1,0:T(8,128)(2,1)} %reduce-scatter.2.cloned.1.call-done), calls=%async_computation.3 | async-start | bytes 1572864 | tf_op jit(solution)/shard_map/all_to_all | solution.py:76
  113.6 0.1 reduce_sum.50
  113.7 0.0 copy-done.1
  113.7 0.1 copy.33
  113.8 0.1 mul.55
  114.0 0.1 copy.29
  114.1 0.1 copy.30
  114.2 0.0 copy-done.2
  114.2 0.1 copy.34
  114.3 19.4 %all-to-all-done.2 = bf16[4,48,2048]{2,1,0:T(8,128)(2,1)S(1)} async-done(((bf16[4,48,2048]{2,1,0:T(8,128)(2,1)}), bf16[4,48,2048]{2,1,0:T(8,128)(2,1)S(1)}, u32[]{:S(2)}, u32[]{:S(2)}) %all-to-all-start.2) | async-done | bytes 786464 | tf_op jit(solution)/shard_map/all_to_all | solution.py:76
  133.7 0.2 bitcast_convert_fusion
  133.9 1.0 gather_fusion
  134.9 0.6 gather.7
  135.5 3.2 %multiply_reduce_fusion = bf16[64,2048]{1,0:T(8,128)(2,1)} fusion(f32[64,2,2048]{2,1,0:T(2,128)S(1)} %gather.7, pred[64,2]{1,0:T(8,128)(4,1)S(1)} %copy.30, f32[64,2]{1,0:T(8,128)S(1)} %copy.34), kind=kLoop, calls=%fused_computation.16 | loop fusion | flops 655360 | bytes 1311360 | tf_op jit(solution)/shard_map/reduce_sum | solution.py:82
  (10 shorter events, 0.1 us)
Async XLA Ops:
  6.5 69.6 %copy-start = (bf16[1,128,768]{2,1,0:T(8,128)(2,1)S(1)}, bf16[1,128,768]{2,1,0:T(8,128)(2,1)}, u32[]{:S(2)}) copy-start(bf16[1,128,768]{2,1,0:T(8,128)(2,1)} %param.17) | copy-start | bytes 589828
  9.6 17.0 %all-to-all-start.1 = ((bf16[4,1,48]{2,1,0:T(2,128)(2,1)}), bf16[4,1,48]{2,1,0:T(2,128)(2,1)S(1)}, u32[]{:S(2)}, u32[]{:S(2)}) async-start(bf16[4,1,48]{2,1,0:T(2,128)(2,1)} %convert_element_type.62), calls=%async_computation.1 | async-start | bytes 4096 | tf_op jit(solution)/shard_map/all_to_all | solution.py:57
  26.7 40.3 %all-to-all-start = ((bf16[4,48,4096]{2,1,0:T(8,128)(2,1)}), bf16[4,48,4096]{2,1,0:T(8,128)(2,1)S(1)}, u32[]{:S(2)}, u32[]{:S(2)}) async-start(bf16[4,48,4096]{2,1,0:T(8,128)(2,1)} %bitcast), calls=%async_computation | async-start | bytes 3145728 | tf_op jit(solution)/shard_map/all_to_all | solution.py:56
  31.5 44.6 %all-gather.3.cloned.1.call-start = ((), (), s32[]{:S(2)}) async-start(), calls=%async_computation.5 | async-start | bytes 1572864 | tf_op jit(solution)/shard_map/all_gather | solution.py:55
  32.2 76.8 %reduce-scatter.2.cloned.1.call-start = ((), (), s32[]{:S(2)}) async-start(), calls=%async_computation.4 | async-start | bytes 2359296 | tf_op jit(solution)/shard_map/reduce_scatter | solution.py:73
  83.6 30.1 %copy-start.1 = (s32[64,2]{0,1:T(2,128)S(1)}, s32[64,2]{0,1:T(2,128)}, u32[]{:S(2)}) copy-start(s32[64,2]{0,1:T(2,128)} %param.10) | copy-start | bytes 1540
  83.6 30.6 %copy-start.2 = (f32[64,2]{0,1:T(2,128)S(1)}, f32[64,2]{0,1:T(2,128)}, u32[]{:S(2)}) copy-start(f32[64,2]{0,1:T(2,128)} %param.11) | copy-start | bytes 1540
  109.0 24.7 %all-to-all-start.2 = ((bf16[4,48,2048]{2,1,0:T(8,128)(2,1)}), bf16[4,48,2048]{2,1,0:T(8,128)(2,1)S(1)}, u32[]{:S(2)}, u32[]{:S(2)}) async-start(bf16[4,48,2048]{2,1,0:T(8,128)(2,1)} %reduce-scatter.2.cloned.1.call-done), calls=%async_computation.3 | async-start | bytes 1572864 | tf_op jit(solution)/shard_map/all_to_all | solution.py:76
Sparse Core Ops, SparseCore 0:
  33.8 22.7 all-gather.2
  83.8 25.1 reduce-scatter.1
where the time goes:
time: 146 us
  waiting for transfers between devices  80 us (55%)
  matrix products  18.7 us (13%)
  starting transfers between devices  15.8 us (11%)
  between operations  13.5 us (9%)
  blocking collectives  8.64 us (6%)
  other arithmetic  4.79 us (3%)
  local copies, waits for them, and re-layouts  4.06 us (3%)
    all_to_all x1, waiting for transfers between devices, local(): lax.all_to_all(send_rows, 'expert', split_axis=0, concat_axis=0, tiled=True)  34.6 us
    reduce_scatter x1, waiting for transfers between devices, local(): lax.psum_scatter(partial_value.astype(jnp.bfloat16), 'hidden', scatter_di...  25.3 us
    all_to_all x1, waiting for transfers between devices, local(): lax.all_to_all(result.astype(jnp.bfloat16), 'expert', split_axis=0, conca...  19.4 us
    all_gather x1, blocking collectives, local(): source_rows = lax.all_gather(tokens, 'hidden', axis=1, tiled=True)  8.64 us
    all_to_all x1, starting transfers between devices, local(): lax.all_to_all(send_codes, 'expert', split_axis=0, concat_axis=0, tiled=T...  6.32 us
    dot_general x1, matrix products, local(): jnp.dot(hidden_act, down_weight[0], preferred_element_type=jnp.float32)  5.34 us
    dot_general x1, matrix products, local(): jnp.dot(flattened, gate_weight[0], preferred_element_type=jnp.float32)  4.98 us
    all_to_all x1, starting transfers between devices, local(): lax.all_to_all(send_rows, 'expert', split_axis=0, concat_axis=0, tiled=True)  4.81 us
  transfers between devices with their start and end apart: 5, of which 3 were waited for; matrix products, arithmetic and copies ran while one was open for 8% of the time, Pallas kernels for 0%

commit v1 on v0

v1 whole, which is shorter than its diff:
```python
import functools

import jax
import jax.numpy as jnp
from jax import lax
from jax.experimental import pallas as pl
from jax.experimental.pallas import tpu as pltpu
from jax.sharding import PartitionSpec as P

RANK = 8
MESH = pl.DeviceIdType.MESH
F32 = jnp.float32
BF16 = jnp.bfloat16


def tile_of(size, most):
    return most if size % most == 0 else size


def dot(a, b):
    return jnp.dot(a, b, preferred_element_type=F32)


def kernel(
    E,
    H,
    cap,
    tok_ref,
    ids_ref,
    wt_ref,
    slot_ref,
    gw_hbm,
    uw_hbm,
    dw_hbm,
    ad_hbm,
    au_hbm,
    out_ref,
    gw,
    uw,
    dw,
    ad,
    au,
    zsend,
    zrecv,
    xrows,
    xrank,
    rank_own,
    rank_out,
    act,
    pout,
    pin,
    yown,
    rbuf,
    ret,
    comb,
    w_sem,
    z_s,
    z_r,
    x_s,
    x_r,
    k_s,
    k_r,
    o_s,
    o_r,
    b_s,
    b_r,
):
    me_e = lax.axis_index("expert")
    me_h = lax.axis_index("hidden")
    T, Dsh = tok_ref.shape
    K = ids_ref.shape[0]
    U = slot_ref.shape[1]
    F = gw.shape[1]
    A = ad.shape[1]

    loads = [
        pltpu.make_async_copy(src.at[0], dst, w_sem.at[i])
        for i, (src, dst) in enumerate(
            ((ad_hbm, ad), (gw_hbm, gw), (uw_hbm, uw), (au_hbm, au), (dw_hbm, dw))
        )
    ]
    for load in loads:
        load.start()

    barrier = pltpu.get_barrier_semaphore()
    for d in range(1, E):
        pl.semaphore_signal(
            barrier, inc=1, device_id={"expert": lax.rem(me_e + d, E)}, device_id_type=MESH
        )
    for j in range(1, H):
        pl.semaphore_signal(
            barrier, inc=1, device_id={"hidden": lax.rem(me_h + j, H)}, device_id_type=MESH
        )

    def z_copy(d):
        return pltpu.make_async_remote_copy(
            src_ref=zsend.at[d],
            dst_ref=zrecv.at[d],
            send_sem=z_s.at[d],
            recv_sem=z_r.at[d],
            device_id={"expert": lax.rem(me_e + d, E)},
            device_id_type=MESH,
        )

    def x_copy(d, j):
        return pltpu.make_async_remote_copy(
            src_ref=zrecv.at[d, :, pl.ds(0, Dsh)],
            dst_ref=xrows.at[j, d],
            send_sem=x_s.at[j, d],
            recv_sem=x_r.at[j, d],
            device_id={"hidden": lax.rem(me_h + j, H)},
            device_id_type=MESH,
        )

    def k_copy(d, j):
        return pltpu.make_async_remote_copy(
            src_ref=rank_out.at[d],
            dst_ref=xrank.at[j, d],
            send_sem=k_s.at[j, d],
            recv_sem=k_r.at[j, d],
            device_id={"hidden": lax.rem(me_h + j, H)},
            device_id_type=MESH,
        )

    def o_copy(d, j):
        return pltpu.make_async_remote_copy(
            src_ref=pout.at[j, d],
            dst_ref=pin.at[j, d],
            send_sem=o_s.at[j, d],
            recv_sem=o_r.at[j, d],
            device_id={"hidden": lax.rem(me_h + j, H)},
            device_id_type=MESH,
        )

    def b_copy(d):
        return pltpu.make_async_remote_copy(
            src_ref=rbuf.at[d],
            dst_ref=ret.at[d],
            send_sem=b_s.at[d],
            recv_sem=b_r.at[d],
            device_id={"expert": lax.rem(me_e - d + E, E)},
            device_id_type=MESH,
        )

    R = max(E, 8)
    ids = ids_ref[...]
    wts = wt_ref[...]
    named = lax.rem(lax.broadcasted_iota(jnp.int32, (R, T), 0) + me_e, E)
    chosen = jnp.zeros((R, T), F32)
    weight = jnp.zeros((R, T), F32)
    for k in range(K):
        hit = ids[k : k + 1, :] == named
        chosen += jnp.where(hit, 1.0, 0.0)
        weight += jnp.where(hit, wts[k : k + 1, :], 0.0)
    before = lax.broadcasted_iota(jnp.int32, (T, T), 0) < lax.broadcasted_iota(
        jnp.int32, (T, T), 1
    )
    place = dot(chosen.astype(BF16), jnp.where(before, 1.0, 0.0).astype(BF16))
    place = jnp.where(chosen > 0.0, place, -1.0)
    row_no = lax.broadcasted_iota(jnp.int32, (cap, T), 0).astype(F32)
    picks = [row_no == place[d : d + 1, :] for d in range(E)]
    select = jnp.concatenate([jnp.where(p, 1.0, 0.0) for p in picks], axis=0).astype(BF16)
    slots = slot_ref[...].astype(F32)
    slot_no = lax.broadcasted_iota(jnp.int32, slots.shape, 0)
    eye = lax.broadcasted_iota(jnp.int32, (U, U), 0) == lax.broadcasted_iota(
        jnp.int32, (U, U), 1
    )
    column_slot = (lax.broadcasted_iota(jnp.int32, (U, A), 1) // RANK).astype(F32)

    def mask_of(d):
        row = jnp.sum(
            jnp.where(slot_no == lax.rem(me_e + d, E), slots, 0.0), axis=0, keepdims=True
        )
        column = jnp.sum(jnp.where(eye, row, 0.0), axis=1, keepdims=True)
        user = jnp.where(column == column_slot, 1.0, 0.0)
        tokens = jnp.broadcast_to(user[:, None, :], (U, T // U, A)).reshape(T, A)
        return dot(select[d * cap : (d + 1) * cap], tokens.astype(BF16)).astype(BF16)

    tok = tok_ref[...]
    picked = dot(select, tok).astype(BF16)
    for d in range(E):
        block = zrecv if d == 0 else zsend
        block[d, :, pl.ds(0, Dsh)] = picked[d * cap : (d + 1) * cap]
        block[d, :, pl.ds(Dsh, A)] = mask_of(d)

    pl.semaphore_wait(barrier, E + H - 2)
    for d in range(1, E):
        z_copy(d).start()

    loads[0].wait()

    def forward(d):
        for j in range(1, H):
            x_copy(d, j).start()
        mine = dot(zrecv[d, :, pl.ds(0, Dsh)], ad[...])
        mine = jnp.where(zrecv[d, :, pl.ds(Dsh, A)] > 0, mine, 0.0)
        rank_own[d] = mine
        rank_out[d] = mine.astype(BF16)
        for j in range(1, H):
            k_copy(d, j).start()

    forward(0)
    scaled = jnp.concatenate(
        [jnp.where(p, weight[d : d + 1, :], 0.0) for d, p in enumerate(picks)], axis=0
    ).T
    high = scaled.astype(BF16)
    comb[pl.ds(0, T), :] = high
    comb[pl.ds(T, T), :] = (scaled - high.astype(F32)).astype(BF16)
    for load in loads[1:]:
        load.wait()

    tf = tile_of(F, 256)
    tn = tile_of(Dsh, 512)

    def compute(d):
        for j in range(1, H):
            x_copy(d, j).wait_recv()
            k_copy(d, j).wait_recv()
        rank = rank_own[d]
        for j in range(1, H):
            rank += xrank[j, d].astype(F32)
        rank = rank.astype(BF16)

        for c in range(F // tf):
            columns = pl.ds(c * tf, tf)
            up = dot(rank, au[:, columns])
            gate = jnp.zeros_like(up)
            for j in range(H):
                rows = pl.ds(pl.multiple_of(lax.rem(me_h - j + H, H) * Dsh, Dsh), Dsh)
                left = zrecv[d, :, pl.ds(0, Dsh)] if j == 0 else xrows[j, d]
                gate += dot(left, gw[rows, columns])
                up += dot(left, uw[rows, columns])
            act[:, columns] = (gate / (1.0 + jnp.exp(-gate)) * up).astype(BF16)

        for j in list(range(1, H)) + [0]:
            start = lax.rem(me_h + j, H) * Dsh

            @pl.loop(0, Dsh // tn)
            def _(c):
                columns = pl.ds(pl.multiple_of(start + c * tn, tn), tn)
                part = dot(act[...], dw[:, columns]).astype(BF16)
                here = pl.ds(pl.multiple_of(c * tn, tn), tn)
                if j == 0:
                    yown[d, :, here] = part
                else:
                    pout[j, d, :, here] = part

            if j:
                o_copy(d, j).start()

    def give_back(d):
        total = yown[d].astype(F32)
        for j in range(1, H):
            o_copy(d, j).wait_recv()
            total += pin[j, d].astype(F32)
        rbuf[d] = total.astype(BF16)

        @pl.when(d > 0)
        def _():
            b_copy(d).start()

    @pl.loop(0, E)
    def _(d):
        @pl.when(d + 1 < E)
        def _():
            z_copy(d + 1).wait_recv()
            forward(d + 1)

        compute(d)

        @pl.when(d > 0)
        def _():
            give_back(d - 1)

    give_back(jnp.int32(E - 1))

    ret[0] = rbuf[0]
    for d in range(1, E):
        b_copy(d).wait_recv()
    both = dot(comb[...], ret[...].reshape(E * cap, Dsh))
    out_ref[...] = (both[:T] + both[T:]).astype(BF16)

    @pl.loop(0, E)
    def _(d):
        for j in range(1, H):
            x_copy(d, j).wait_send()
            k_copy(d, j).wait_send()
            o_copy(d, j).wait_send()

        @pl.when(d > 0)
        def _():
            z_copy(d).wait_send()
            b_copy(d).wait_send()


def local(
    tokens,
    route_ids,
    route_weight,
    user_slot,
    gate_weight,
    up_weight,
    down_weight,
    adapter_down,
    adapter_up,
):
    E = lax.axis_size("expert")
    H = lax.axis_size("hidden")
    T, K = route_ids.shape
    cap = T * K * 3 // (2 * E)
    Dsh = tokens.shape[1]
    D = gate_weight.shape[1]
    F = gate_weight.shape[2]
    A = adapter_down.shape[2]
    vmem = pl.BlockSpec(memory_space=pltpu.VMEM)
    hbm = pl.BlockSpec(memory_space=pl.ANY)
    dma = pltpu.SemaphoreType.DMA
    rows = E * cap
    flops = 2 * rows * (3 * D * F + Dsh * A + A * F)
    return pl.pallas_call(
        functools.partial(kernel, E, H, cap),
        out_shape=jax.ShapeDtypeStruct((T, Dsh), BF16),
        in_specs=[vmem] * 4 + [hbm] * 5,
        out_specs=vmem,
        scratch_shapes=[
            pltpu.VMEM((D, F), BF16),
            pltpu.VMEM((D, F), BF16),
            pltpu.VMEM((F, D), BF16),
            pltpu.VMEM((Dsh, A), BF16),
            pltpu.VMEM((A, F), BF16),
            pltpu.VMEM((E, cap, Dsh + A), BF16),
            pltpu.VMEM((E, cap, Dsh + A), BF16),
            pltpu.VMEM((H, E, cap, Dsh), BF16),
            pltpu.VMEM((H, E, cap, A), BF16),
            pltpu.VMEM((E, cap, A), F32),
            pltpu.VMEM((E, cap, A), BF16),
            pltpu.VMEM((cap, F), BF16),
            pltpu.VMEM((H, E, cap, Dsh), BF16),
            pltpu.VMEM((H, E, cap, Dsh), BF16),
            pltpu.VMEM((E, cap, Dsh), BF16),
            pltpu.VMEM((E, cap, Dsh), BF16),
            pltpu.VMEM((E, cap, Dsh), BF16),
            pltpu.VMEM((2 * T, rows), BF16),
            dma((5,)),
            dma((E,)),
            dma((E,)),
            dma((H, E)),
            dma((H, E)),
            dma((H, E)),
            dma((H, E)),
            dma((H, E)),
            dma((H, E)),
            dma((E,)),
            dma((E,)),
        ],
        compiler_params=pltpu.CompilerParams(
            collective_id=0, has_side_effects=True, vmem_limit_bytes=56 * 1024 * 1024
        ),
        cost_estimate=pl.CostEstimate(
            flops=flops, bytes_accessed=6 * D * F, transcendentals=rows * F
        ),
    )(
        tokens,
        route_ids.T,
        route_weight.T,
        user_slot.T,
        gate_weight,
        up_weight,
        down_weight,
        adapter_down,
        adapter_up,
    )


def solution(mesh):
    in_specs = (
        P(("parts", "expert", "rep"), "hidden"),
        P(("parts", "expert", "rep"), None),
        P(("parts", "expert", "rep"), None),
        P(("parts", "expert", "rep"), None),
        P("expert", None, "hidden"),
        P("expert", None, "hidden"),
        P("expert", "hidden", None),
        P("expert", "hidden", None),
        P("expert", None, "hidden"),
    )
    out_specs = P(("parts", "expert", "rep"), "hidden")
    return jax.shard_map(local, mesh=mesh, in_specs=in_specs, out_specs=out_specs, check_vma=False)
```

time: 146 us -> 60 us (0.41)
  waiting for transfers between devices: 80 us -> 0 us
  Pallas kernels: 0 us -> 58.2 us
  matrix products: 18.7 us -> 0 us
  starting transfers between devices: 15.8 us -> 0 us
  between operations: 13.5 us -> 0.01 us
  blocking collectives: 8.64 us -> 0 us
  other arithmetic: 4.79 us -> 0 us
  local copies, waits for them, and re-layouts: 4.06 us -> 1.67 us
    pallas_call x0 -> x1, Pallas kernels: none -> 58.2 us  [local(): pl.pallas_call(functools.partial(kernel, E, H, cap), out_shape=jax.ShapeD...]
    all_to_all x3 -> x0, waiting for transfers between devices: 54 us -> none  [the longest x1 34.6 us: local(): lax.all_to_all(send_rows, 'expert', split_axis=0, concat_axis=0, tiled=True)]
    reduce_scatter x1 -> x0, waiting for transfers between devices: 25.3 us -> none  [local(): lax.psum_scatter(partial_value.astype(jnp.bfloat16), 'hidden', scatter_di...]
    dot_general x5 -> x0, matrix products: 18.7 us -> none  [the longest x1 5.34 us: local(): jnp.dot(hidden_act, down_weight[0], preferred_element_type=jnp.float32)]
    all_to_all x3 -> x0, starting transfers between devices: 15.7 us -> none  [the longest x1 6.32 us: local(): lax.all_to_all(send_codes, 'expert', split_axis=0, concat_axis=0, tiled=T...]
    all_gather x1 -> x0, blocking collectives: 8.64 us -> none  [local(): source_rows = lax.all_gather(tokens, 'hidden', axis=1, tiled=True)]
    reduce_sum x4 -> x0, other arithmetic: 4.24 us -> none  [the longest x1 3.18 us: local(): mixed = jnp.sum(picked * route_weight[:, :, None], axis=1)]
    gather x2 -> x0, local copies, waits for them, and re-layouts: 1.6 us -> none  [local(): jnp.take(returned.reshape(experts * expert_capacity, shard_width), slot_i...]
  transfers between devices with their start and end apart: 5 -> 0, of which waited for: 3 -> 0; matrix products, arithmetic and copies ran while one was open for 8% -> 0% of each run, Pallas kernels for 0% -> 0%
where the time goes in v1:
time: 60 us; the launch traced here: 59.9 us
  Pallas kernels  58.2 us (97%)
  local copies, waits for them, and re-layouts  1.67 us (3%)
    pallas_call x1, Pallas kernels, local(): pl.pallas_call(functools.partial(kernel, E, H, cap), out_shape=jax.ShapeD...  58.2 us
    unnamed x1, local copies, waits for them, and re-layouts  1.67 us

profile of v1, /device:TPU:0, one launch (start us, length us, event | category | flops | bytes accessed | tf_op | source)
XLA Modules:
  0.0 59.9 jit_solution(7793426585097882223)
XLA Ops:
  0.0 58.2 %shard_map.91 = bf16[64,2048]{1,0:T(8,128)(2,1)} custom-call(bf16[64,2048]{1,0:T(8,128)(2,1)} %tok_ref.1, s32[2,64]{1,0:T(2,128)} %bitcast.4, f32[2,64]{1,0:T(2,128)} %bitcast.5, s32[4,8]{1,0:T(4,128)} %bitcast.3, bf16[1,4096,768]{2,1,0:T(8,128)(2,1)} %gw_hbm.1, bf16[1,4096,768]{2,1,0:T(8,128)(2,1)} %uw_hbm.1, bf16[1,768,4096]{2,1,0:T(8,128)(2,1)} %dw_hbm.1, ...), custom_call_target="tpu_custom_call" | custom-call | flops 3762290688 | bytes 18874368 | tf_op jit(solution)/shard_map/pallas_call | solution.py:320
  58.2 1.7 %copy.11 = bf16[64,2048]{1,0:T(8,128)(2,1)} copy(bf16[64,2048]{1,0:T(8,128)(2,1)} %shard_map.91) | data formatting | bytes 524288

commit v2 on v1

--- a/solution.py
+++ b/solution.py
@@ -17,6 +17,15 @@
     return most if size % most == 0 else size
 
 
+def partner(me, d, size):
+    bit, other = 1, me
+    while bit < size:
+        if d & bit:
+            other = other + bit - 2 * bit * lax.rem(lax.div(me, jnp.int32(bit)), 2)
+        bit *= 2
+    return other
+
+
 def dot(a, b):
     return jnp.dot(a, b, preferred_element_type=F32)
 
@@ -24,6 +33,7 @@
 def kernel(
     E,
     H,
+    C,
     cap,
     tok_ref,
     ids_ref,
@@ -72,6 +82,10 @@
     U = slot_ref.shape[1]
     F = gw.shape[1]
     A = ad.shape[1]
+    W = Dsh // C
+
+    def piece(c):
+        return pl.ds(c * W, W)
 
     loads = [
         pltpu.make_async_copy(src.at[0], dst, w_sem.at[i])
@@ -85,29 +99,30 @@
     barrier = pltpu.get_barrier_semaphore()
     for d in range(1, E):
         pl.semaphore_signal(
-            barrier, inc=1, device_id={"expert": lax.rem(me_e + d, E)}, device_id_type=MESH
+            barrier, inc=1, device_id={"expert": partner(me_e, d, E)}, device_id_type=MESH
         )
     for j in range(1, H):
         pl.semaphore_signal(
             barrier, inc=1, device_id={"hidden": lax.rem(me_h + j, H)}, device_id_type=MESH
         )
 
-    def z_copy(d):
+    def z_copy(d, c):
+        part = pl.ds(c * W, W + (A if c == C - 1 else 0))
         return pltpu.make_async_remote_copy(
-            src_ref=zsend.at[d],
-            dst_ref=zrecv.at[d],
-            send_sem=z_s.at[d],
-            recv_sem=z_r.at[d],
-            device_id={"expert": lax.rem(me_e + d, E)},
+            src_ref=zsend.at[d, :, part],
+            dst_ref=zrecv.at[d, :, part],
+            send_sem=z_s.at[d, c],
+            recv_sem=z_r.at[d, c],
+            device_id={"expert": partner(me_e, d, E)},
             device_id_type=MESH,
         )
 
-    def x_copy(d, j):
+    def x_copy(d, j, c):
         return pltpu.make_async_remote_copy(
-            src_ref=zrecv.at[d, :, pl.ds(0, Dsh)],
-            dst_ref=xrows.at[j, d],
-            send_sem=x_s.at[j, d],
-            recv_sem=x_r.at[j, d],
+            src_ref=zrecv.at[d, :, piece(c)],
+            dst_ref=xrows.at[j, d, :, piece(c)],
+            send_sem=x_s.at[j, d, c],
+            recv_sem=x_r.at[j, d, c],
             device_id={"hidden": lax.rem(me_h + j, H)},
             device_id_type=MESH,
         )
@@ -122,30 +137,33 @@
             device_id_type=MESH,
         )
 
-    def o_copy(d, j):
+    def o_copy(d, j, c):
         return pltpu.make_async_remote_copy(
-            src_ref=pout.at[j, d],
-            dst_ref=pin.at[j, d],
-            send_sem=o_s.at[j, d],
-            recv_sem=o_r.at[j, d],
+            src_ref=pout.at[j, d, :, piece(c)],
+            dst_ref=pin.at[j, d, :, piece(c)],
+            send_sem=o_s.at[j, d, c],
+            recv_sem=o_r.at[j, d, c],
             device_id={"hidden": lax.rem(me_h + j, H)},
             device_id_type=MESH,
         )
 
-    def b_copy(d):
+    def b_copy(d, c):
         return pltpu.make_async_remote_copy(
-            src_ref=rbuf.at[d],
-            dst_ref=ret.at[d],
-            send_sem=b_s.at[d],
-            recv_sem=b_r.at[d],
-            device_id={"expert": lax.rem(me_e - d + E, E)},
+            src_ref=rbuf.at[d, :, piece(c)],
+            dst_ref=ret.at[d, :, piece(c)],
+            send_sem=b_s.at[d, c],
+            recv_sem=b_r.at[d, c],
+            device_id={"expert": partner(me_e, d, E)},
             device_id_type=MESH,
         )
 
     R = max(E, 8)
     ids = ids_ref[...]
     wts = wt_ref[...]
-    named = lax.rem(lax.broadcasted_iota(jnp.int32, (R, T), 0) + me_e, E)
+    turn = lax.broadcasted_iota(jnp.int32, (R, T), 0)
+    named = jnp.full((R, T), -1, jnp.int32)
+    for d in range(E):
+        named = jnp.where(turn == d, partner(me_e, d, E), named)
     chosen = jnp.zeros((R, T), F32)
     weight = jnp.zeros((R, T), F32)
     for k in range(K):
@@ -169,7 +187,7 @@
 
     def mask_of(d):
         row = jnp.sum(
-            jnp.where(slot_no == lax.rem(me_e + d, E), slots, 0.0), axis=0, keepdims=True
+            jnp.where(slot_no == partner(me_e, d, E), slots, 0.0), axis=0, keepdims=True
         )
         column = jnp.sum(jnp.where(eye, row, 0.0), axis=1, keepdims=True)
         user = jnp.where(column == column_slot, 1.0, 0.0)
@@ -185,13 +203,17 @@
 
     pl.semaphore_wait(barrier, E + H - 2)
     for d in range(1, E):
-        z_copy(d).start()
+        for c in range(C):
+            z_copy(d, c).start()
 
     loads[0].wait()
 
     def forward(d):
-        for j in range(1, H):
-            x_copy(d, j).start()
+        for c in range(C):
+            if d:
+                z_copy(d, c).wait_recv()
+            for j in range(1, H):
+                x_copy(d, j, c).start()
         mine = dot(zrecv[d, :, pl.ds(0, Dsh)], ad[...])
         mine = jnp.where(zrecv[d, :, pl.ds(Dsh, A)] > 0, mine, 0.0)
         rank_own[d] = mine
@@ -210,11 +232,12 @@
         load.wait()
 
     tf = tile_of(F, 256)
-    tn = tile_of(Dsh, 512)
+    tn = tile_of(W, 512)
 
     def compute(d):
         for j in range(1, H):
-            x_copy(d, j).wait_recv()
+            for c in range(C):
+                x_copy(d, j, c).wait_recv()
             k_copy(d, j).wait_recv()
         rank = rank_own[d]
         for j in range(1, H):
@@ -232,65 +255,69 @@
                 up += dot(left, uw[rows, columns])
             act[:, columns] = (gate / (1.0 + jnp.exp(-gate)) * up).astype(BF16)
 
-        for j in list(range(1, H)) + [0]:
-            start = lax.rem(me_h + j, H) * Dsh
-
-            @pl.loop(0, Dsh // tn)
-            def _(c):
-                columns = pl.ds(pl.multiple_of(start + c * tn, tn), tn)
+        def down(j, c):
+            start = lax.rem(me_h + j, H) * Dsh + c * W
+
+            @pl.loop(0, W // tn)
+            def _(n):
+                columns = pl.ds(pl.multiple_of(start + n * tn, tn), tn)
                 part = dot(act[...], dw[:, columns]).astype(BF16)
-                here = pl.ds(pl.multiple_of(c * tn, tn), tn)
+                here = pl.ds(pl.multiple_of(c * W + n * tn, tn), tn)
                 if j == 0:
                     yown[d, :, here] = part
                 else:
                     pout[j, d, :, here] = part
 
             if j:
-                o_copy(d, j).start()
+                o_copy(d, j, c).start()
+
+        for j in range(1, H):
+            for c in range(C):
+                down(j, c)
+        for c in range(C):
+            down(0, c)
 
     def give_back(d):
-        total = yown[d].astype(F32)
+        for c in range(C):
+            total = yown[d, :, piece(c)].astype(F32)
+            for j in range(1, H):
+                o_copy(d, j, c).wait_recv()
+                total += pin[j, d, :, piece(c)].astype(F32)
+            if d:
+                rbuf[d, :, piece(c)] = total.astype(BF16)
+                b_copy(d, c).start()
+            else:
+                ret[0, :, piece(c)] = total.astype(BF16)
+
+    for d in range(1, E):
+        forward(d)
+        if d > 1:
+            compute(d - 1)
+        if d > 2:
+            give_back(d - 2)
+    compute(E - 1)
+    if E > 2:
+        give_back(E - 2)
+    compute(0)
+    give_back(E - 1)
+    give_back(0)
+
+    for c in range(C):
+        for d in range(1, E):
+            b_copy(d, c).wait_recv()
+        both = dot(comb[...], ret[:, :, piece(c)].reshape(E * cap, W))
+        out_ref[:, piece(c)] = (both[:T] + both[T:]).astype(BF16)
+
+    for d in range(E):
         for j in range(1, H):
-            o_copy(d, j).wait_recv()
-            total += pin[j, d].astype(F32)
-        rbuf[d] = total.astype(BF16)
-
-        @pl.when(d > 0)
-        def _():
-            b_copy(d).start()
-
-    @pl.loop(0, E)
-    def _(d):
-        @pl.when(d + 1 < E)
-        def _():
-            z_copy(d + 1).wait_recv()
-            forward(d + 1)
-
-        compute(d)
-
-        @pl.when(d > 0)
-        def _():
-            give_back(d - 1)
-
-    give_back(jnp.int32(E - 1))
-
-    ret[0] = rbuf[0]
-    for d in range(1, E):
-        b_copy(d).wait_recv()
-    both = dot(comb[...], ret[...].reshape(E * cap, Dsh))
-    out_ref[...] = (both[:T] + both[T:]).astype(BF16)
-
-    @pl.loop(0, E)
-    def _(d):
-        for j in range(1, H):
-            x_copy(d, j).wait_send()
+            for c in range(C):
+                x_copy(d, j, c).wait_send()
+                o_copy(d, j, c).wait_send()
             k_copy(d, j).wait_send()
-            o_copy(d, j).wait_send()
-
-        @pl.when(d > 0)
-        def _():
-            z_copy(d).wait_send()
-            b_copy(d).wait_send()
+        if d:
+            for c in range(C):
+                z_copy(d, c).wait_send()
+                b_copy(d, c).wait_send()
 
 
 def local(
@@ -316,9 +343,10 @@
     hbm = pl.BlockSpec(memory_space=pl.ANY)
     dma = pltpu.SemaphoreType.DMA
     rows = E * cap
+    C = 2 if Dsh % 1024 == 0 else 1
     flops = 2 * rows * (3 * D * F + Dsh * A + A * F)
     return pl.pallas_call(
-        functools.partial(kernel, E, H, cap),
+        functools.partial(kernel, E, H, C, cap),
         out_shape=jax.ShapeDtypeStruct((T, Dsh), BF16),
         in_specs=[vmem] * 4 + [hbm] * 5,
         out_specs=vmem,
@@ -342,16 +370,16 @@
             pltpu.VMEM((E, cap, Dsh), BF16),
             pltpu.VMEM((2 * T, rows), BF16),
             dma((5,)),
-            dma((E,)),
-            dma((E,)),
+            dma((E, C)),
+            dma((E, C)),
+            dma((H, E, C)),
+            dma((H, E, C)),
             dma((H, E)),
             dma((H, E)),
-            dma((H, E)),
-            dma((H, E)),
-            dma((H, E)),
-            dma((H, E)),
-            dma((E,)),
-            dma((E,)),
+            dma((H, E, C)),
+            dma((H, E, C)),
+            dma((E, C)),
+            dma((E, C)),
         ],
         compiler_params=pltpu.CompilerParams(
             collective_id=0, has_side_effects=True, vmem_limit_bytes=56 * 1024 * 1024

time: 60 us -> 54 us (0.900)
  Pallas kernels: 58.2 us -> 52.2 us
    pallas_call x1, Pallas kernels: 58.2 us -> 52.2 us  [local(): pl.pallas_call(functools.partial(kernel, E, H, C, cap), out_shape=jax.Sha...]
where the time goes in v2:
time: 54 us; the launch traced here: 53.9 us
  Pallas kernels  52.2 us (97%)
  local copies, waits for them, and re-layouts  1.67 us (3%)
    pallas_call x1, Pallas kernels, local(): pl.pallas_call(functools.partial(kernel, E, H, C, cap), out_shape=jax.Sha...  52.2 us
    unnamed x1, local copies, waits for them, and re-layouts  1.67 us

profile of v2, /device:TPU:0, one launch (start us, length us, event | category | flops | bytes accessed | tf_op | source)
XLA Modules:
  0.0 53.9 jit_solution(8393295223923203485)
XLA Ops:
  0.0 52.2 %shard_map.91 = bf16[64,2048]{1,0:T(8,128)(2,1)} custom-call(bf16[64,2048]{1,0:T(8,128)(2,1)} %tok_ref.1, s32[2,64]{1,0:T(2,128)} %bitcast.4, f32[2,64]{1,0:T(2,128)} %bitcast.5, s32[4,8]{1,0:T(4,128)} %bitcast.3, bf16[1,4096,768]{2,1,0:T(8,128)(2,1)} %gw_hbm.1, bf16[1,4096,768]{2,1,0:T(8,128)(2,1)} %uw_hbm.1, bf16[1,768,4096]{2,1,0:T(8,128)(2,1)} %dw_hbm.1, ...), custom_call_target="tpu_custom_call" | custom-call | flops 3762290688 | bytes 18874368 | tf_op jit(solution)/shard_map/pallas_call | solution.py:348
  52.2 1.7 %copy.11 = bf16[64,2048]{1,0:T(8,128)(2,1)} copy(bf16[64,2048]{1,0:T(8,128)(2,1)} %shard_map.91) | data formatting | bytes 524288
